TPU v7x, 32 devices: a whole 2x2x4 slice. The times are simulated.
32 devices in a mesh: seq: 4 (over x, core), head: 4 (over z), batch: 2 (over y).
Axes of the slice: x: 2, y: 2, z: 4, core: 2. Of those that a mesh axis runs over, the one named last changes fastest.
Arguments:
- hyena_inputs: bfloat16 [4096, 3, 8192], P(('batch', 'seq'), None, 'head'), parts along dimension 0, may hold values from -6 to 6
- short_filter: float32 [3, 3, 8192], P(None, None, 'head'), may hold values from -3.5 to 3.5
- medium_filter: float32 [128, 8192], P(None, 'head'), may hold values from -0.5 to 0.5
- q_proj: bfloat16 [4096, 8192], P(('batch', 'seq'), 'head'), parts along dimension 0, may hold values from -8 to 8
- k_proj: bfloat16 [4096, 8192], P(('batch', 'seq'), 'head'), parts along dimension 0, may hold values from -8 to 8
- out_weight: bfloat16 [8192, 8192], P('head'), may hold values from -0.25 to 0.25
Outputs:
- hyena_out: bfloat16 [4096, 8192], P(('batch', 'seq'), 'head'), parts along dimension 0
- mixed: bfloat16 [4096, 8192], P(('batch', 'seq'), 'head'), parts along dimension 0
There are 2 independent parts, one for each index of `batch`. A program takes and returns all parts, laid end to end along the dimension named above; an argument that names none is the same for every part. Nothing has to cross between parts.
All inputs are finite; a program needn't handle non-finite values.
Results may differ from a plain program's by a relative error of at most 0.011.
Values may be sent and summed in bfloat16 or wider, within the bound.
A program may use at most 192 MiB of HBM per device.

v0:
```python
import math
import jax
import jax.numpy as jnp
from jax import lax
from jax.sharding import PartitionSpec as P

HEAD_SIZE = 128


def passed_along(x, axis, by):
    length = lax.axis_size(axis)
    pairs = [(i, i + by) for i in range(length) if 0 <= i + by < length]
    return lax.ppermute(x, axis, pairs)


def causal_depthwise(extended, taps, out_rows):
    tap_count = taps.shape[0]
    window = extended[extended.shape[0] - out_rows - tap_count + 1 :]
    kernel = taps[::-1][:, None, :]
    result = lax.conv_general_dilated(
        window[None],
        kernel,
        (1,),
        "VALID",
        feature_group_count=extended.shape[1],
        dimension_numbers=("NWC", "WIO", "NWC"),
        precision=lax.Precision.HIGHEST,
    )
    return result[0]


def per_device(hyena_inputs, short_filter, medium_filter, q_proj, k_proj, out_weight):
    tok_rows = hyena_inputs.shape[0]
    chan_width = hyena_inputs.shape[2]
    short_taps = short_filter.shape[1]
    med_taps = medium_filter.shape[0]
    short_table = jnp.transpose(short_filter, (1, 0, 2)).reshape(short_taps, 3 * chan_width)
    input_margin = passed_along(hyena_inputs[tok_rows - (short_taps - 1) :], "seq", 1)
    joined = (
        jnp.concatenate([input_margin, hyena_inputs], 0)
        .astype(jnp.float32)
        .reshape(-1, 3 * chan_width)
    )
    filtered = causal_depthwise(joined, short_table, tok_rows).reshape(tok_rows, 3, chan_width)
    product = (filtered[:, 1] * filtered[:, 2]).astype(jnp.bfloat16)
    product_margin = passed_along(product[tok_rows - (med_taps - 1) :], "seq", 1)
    product_ext = jnp.concatenate([product_margin, product], 0)
    medium = causal_depthwise(product_ext.astype(jnp.float32), medium_filter, tok_rows)
    hyena_out = (filtered[:, 0] * medium).astype(jnp.bfloat16)
    head_count = chan_width // HEAD_SIZE
    score_scale = HEAD_SIZE ** (-0.5)
    seq_index = lax.axis_index("seq")
    queries = q_proj.reshape(tok_rows, head_count, HEAD_SIZE)
    query_pos = seq_index * tok_rows + jnp.arange(tok_rows, dtype=jnp.int32)
    last_query = seq_index * tok_rows + tok_rows - 1
    initial = (
        jnp.zeros((head_count, tok_rows, HEAD_SIZE), jnp.float32),
        jnp.full((head_count, tok_rows), -1e30, jnp.float32),
        jnp.zeros((head_count, tok_rows), jnp.float32),
    )
    carried = initial
    first_row = jnp.int32(0)
    key_piece = lax.all_gather(k_proj, "seq", axis=0, tiled=True)
    value_piece = lax.all_gather(hyena_out, "seq", axis=0, tiled=True)
    piece_rows = key_piece.shape[0]
    block_rows = math.gcd(piece_rows, 512)
    block_count = piece_rows // block_rows
    key_blocks = key_piece.reshape(block_count, block_rows, head_count, HEAD_SIZE)
    value_blocks = value_piece.reshape(block_count, block_rows, head_count, HEAD_SIZE)

    def visit(running, block_item):
        key_blk, value_blk, block_number = block_item
        key_start = first_row + block_number * block_rows

        def attend(current):
            weighted, run_max, total_sum = current
            scores = (
                jnp.einsum("qhd,khd->hqk", queries, key_blk, preferred_element_type=jnp.float32)
                * score_scale
            )
            key_pos = key_start + jnp.arange(block_rows, dtype=jnp.int32)
            allowed = key_pos[None, None, :] <= query_pos[None, :, None]
            masked = jnp.where(allowed, scores, -jnp.inf)
            new_max = jnp.maximum(run_max, jnp.max(masked, axis=-1))
            weights = jnp.exp(masked - new_max[..., None])
            factor = jnp.exp(run_max - new_max)
            new_total = total_sum * factor + jnp.sum(weights, axis=-1)
            new_weighted = weighted * factor[..., None] + jnp.einsum(
                "hqk,khd->hqd",
                weights.astype(jnp.bfloat16),
                value_blk,
                preferred_element_type=jnp.float32,
            )
            return (new_weighted, new_max, new_total)

        def keep_state(current):
            return current

        return (lax.cond(key_start <= last_query, attend, keep_state, running), None)

    carried, unused = lax.scan(
        visit, carried, (key_blocks, value_blocks, jnp.arange(block_count, dtype=jnp.int32))
    )
    weighted, run_max, total_sum = carried
    attended = (
        (weighted / total_sum[..., None])
        .transpose(1, 0, 2)
        .reshape(tok_rows, chan_width)
        .astype(jnp.bfloat16)
    )
    summed = lax.psum_scatter(
        lax.dot_general(
            out_weight, attended, (((0,), (1,)), ((), ())), preferred_element_type=jnp.float32
        ).astype(jnp.bfloat16),
        "head",
        scatter_dimension=0,
        tiled=True,
    ).astype(jnp.float32)
    return (hyena_out, summed.T.astype(jnp.bfloat16))


def solution(mesh):
    return jax.shard_map(
        per_device,
        mesh=mesh,
        in_specs=(
            P(("batch", "seq"), None, "head"),
            P(None, None, "head"),
            P(None, "head"),
            P(("batch", "seq"), "head"),
            P(("batch", "seq"), "head"),
            P("head", None),
        ),
        out_specs=(P(("batch", "seq"), "head"), P(("batch", "seq"), "head")),
        check_vma=False,
    )
```

profile of v0, /device:TPU:0, one launch (start us, length us, event | category | flops | bytes accessed | tf_op | source)
XLA Modules:
  0.0 636.0 jit_solution(6922452532543686896)
XLA Ops:
  10.6 16.9 %rev.6 = f32[3,6144]{1,0:T(4,128)S(1)} reverse(f32[3,6144]{1,0:T(4,128)} %bitcast.76), dimensions={0} | reverse | bytes 147456 | tf_op jit(solution)/shard_map/rev | solution.py:19
  27.6 7.8 %pad_maximum_fusion = bf16[514,3,2048]{2,0,1:T(8,128)(2,1)} fusion(bf16[512,3,2048]{2,0,1:T(8,128)(2,1)} %param.10, bf16[2,3,2048]{2,0,1:T(2,128)(2,1)S(1)} %collective-permute-done), kind=kLoop, calls=%fused_computation.37 | loop fusion | flops 12632064 | bytes 12632064 | tf_op jit(solution)/shard_map/concatenate | solution.py:40
  35.4 9.7 %copy.12 = bf16[514,3,2048]{0,2,1:T(8,128)(2,1)} copy(bf16[514,3,2048]{2,0,1:T(8,128)(2,1)} %pad_maximum_fusion) | data formatting | bytes 12632064 | tf_op jit(solution)/shard_map/concatenate | solution.py:40
  52.1 20.5 %reshape.76 = bf16[1,8,65,6144]{2,1,3,0:T(8,128)(2,1)} reshape(bf16[1,520,6144]{1,2,0:T(8,128)(2,1)} %pad) | data formatting | bytes 12779520 | tf_op jit(solution)/shard_map/conv_general_dilated | solution.py:20
  72.7 16.8 %copy.15 = bf16[1,8,65,6144]{3,1,2,0:T(8,128)(2,1)} copy(bf16[1,8,65,6144]{2,1,3,0:T(8,128)(2,1)} %reshape.76) | data formatting | bytes 12779520 | tf_op jit(solution)/shard_map/conv_general_dilated | solution.py:20
  90.4 11.8 %fusion.30 = f32[8,65,6144]{2,0,1:T(8,128)} fusion(f32[3,1,6144]{2,1,0:T(1,128)S(1)} %broadcast_in_dim.40, bf16[1,7,2,6144]{3,1,2,0:T(8,128)(2,1)S(1)} %slice.26, bf16[1,8,65,6144]{3,1,2,0:T(8,128)(2,1)} %copy.15, pred[8,65]{0,1:T(8,128)(4,1)S(1)} %copy-done.4), kind=kOutput, calls=%fused_computation.33 | convolution fusion | flops 137969664 | bytes 19415560 | tf_op jit(solution)/shard_map/conv_general_dilated | solution.py:20
  102.2 17.2 %copy.16 = f32[8,65,6144]{2,1,0:T(8,128)} copy(f32[8,65,6144]{2,0,1:T(8,128)} %fusion.30) | data formatting | bytes 25559040 | tf_op jit(solution)/shard_map/conv_general_dilated | solution.py:20
  119.4 11.3 %reshape.72 = f32[1,520,6144]{2,1,0:T(8,128)} reshape(f32[8,65,6144]{2,1,0:T(8,128)} %copy.16) | data formatting | bytes 25559040 | tf_op jit(solution)/shard_map/conv_general_dilated | solution.py:20
  130.7 10.6 %slice.27 = f32[1,512,6144]{2,1,0:T(8,128)} slice(f32[1,520,6144]{2,1,0:T(8,128)} %reshape.72), slice={[0:1], [0:512], [0:6144]} | slice | bytes 25165824 | tf_op jit(solution)/shard_map/conv_general_dilated | solution.py:20
  141.3 12.8 %copy.17 = f32[1,512,6144]{1,2,0:T(8,128)} copy(f32[1,512,6144]{2,1,0:T(8,128)} %slice.27) | data formatting | bytes 25165824 | tf_op jit(solution)/shard_map/conv_general_dilated | solution.py:20
  182.8 11.5 %copy.20 = bf16[1,639,2048]{2,0,1:T(2,128)(2,1)} copy(bf16[1,639,2048]{1,2,0:T(8,128)(2,1)} %maximum_bitcast_fusion) | data formatting | bytes 5234688 | tf_op jit(solution)/shard_map/broadcast_in_dim | solution.py:21
  194.4 48.5 %fusion.39 = f32[1,512,2048]{2,0,1:T(1,128)S(1)} fusion(bf16[1,639,2048]{2,0,1:T(2,128)(2,1)} %copy.20, f32[128,1,2048]{2,0,1:T(8,128)S(1)} %bitcast.75), kind=kOutput, calls=%fused_computation.45 | convolution fusion | flops 1610612736 | bytes 7860224 | tf_op jit(solution)/shard_map/conv_general_dilated | solution.py:20
  251.5 10.9 %copy.34 = bf16[256,8,16,128]{3,2,1,0:T(8,128)(2,1)} copy(bf16[256,8,16,128]{3,1,2,0:T(8,128)(2,1)} %bitcast.71) | data formatting | bytes 16777216
  262.3 8.8 %copy.23 = bf16[4,512,16,128]{3,1,2,0:T(8,128)(2,1)} copy(bf16[4,512,16,128]{3,2,1,0:T(8,128)(2,1)} %bitcast.67) | data formatting | bytes 16777216
  271.2 33.2 %all-gather.5.cloned.1.call-done = bf16[2048,2048]{1,0:T(8,128)(2,1)} async-done(((bf16[512,2048]{1,0:T(8,128)(2,1)}), bf16[2048,2048]{1,0:T(8,128)(2,1)}) %all-gather.5.cloned.1.call-update) | async-done | bytes 8388624 | tf_op jit(solution)/shard_map/all_gather | solution.py:64
  304.4 9.8 %copy.35 = bf16[256,8,16,128]{3,2,1,0:T(8,128)(2,1)} copy(bf16[256,8,16,128]{3,1,2,0:T(8,128)(2,1)} %bitcast.72) | data formatting | bytes 16777216
  314.1 8.8 %copy.25 = bf16[4,512,16,128]{3,1,2,0:T(8,128)(2,1)} copy(bf16[4,512,16,128]{3,2,1,0:T(8,128)(2,1)} %bitcast.68) | data formatting | bytes 16777216
  325.4 35.2 %while.15 = (s32[]{:T(128)}, f32[16,512,128]{2,1,0:T(8,128)}, f32[16,512]{1,0:T(8,128)S(1)}, f32[16,512]{1,0:T(8,128)S(1)}, s32[4]{0:T(128)S(1)}, /*index=5*/s32...) while((s32[]{:T(128)}, f32[16,512,128]{2,1,0:T(8,128)}, ...), condition=%wide.region_5.6_spmd.clone, body=%wide.region_0.5_spmd.clone.sunk | while | flops 2195997696 | bytes 66598184 | solution.py:101
  326.9 30.0 %conditional.3 = ((f32[16,512,128]{2,1,0:T(8,128)}, f32[16,512]{1,0:T(8,128)S(1)}, f32[16,512]{1,0:T(8,128)S(1)})) conditional(s32[]{:T(128)} %convert_element_type.60, (f32[16,512,128]{2,1,0:T(8,128)}, f32[16,512]{1,0:T(8,128)S(1)}, f32[16,512]{1,0:T(8,128)S(1)}) %tuple.46, (s32[]{:T(128)}, s32[]{:T(128)}, bf16[4,512,16,128]{3,1,2,0:T(8,128)(2,1)}, ...), branch_computations={%region_1.1_spmd, %region_2.4_spmd} | conditional | flops 2195997696 | bytes 66595880 | solution.py:99
  327.1 8.8 %fusion.4 = (f32[16,512]{1,0:T(8,128)S(1)}, f32[16,512,512]{2,1,0:T(8,128)}) fusion(pred[512,512]{0,1:T(8,128)(4,1)S(1)} %broadcast_compare_fusion, bf16[512,16,128]{2,0,1:T(8,128)(2,1)S(1)} %get-tuple-element.117, bf16[4,512,16,128]{3,1,2,0:T(8,128)(2,1)} %get-tuple-element.115, s32[]{:T(128)} %get-tuple-element.116), kind=kOutput, calls=%fused_computation.5 | convolution fusion | flops 1086316544 | bytes 21266944 | tf_op jit(solution)/shard_map/while/body/eval_jaxpr/cond/branch_1_fun/qhd,khd->hqk/dot_general | solution.py:78
  335.9 9.1 %fusion.2 = f32[16,512]{1,0:T(8,128)S(1)} fusion(f32[16,512,512]{2,1,0:T(8,128)} %get-tuple-element.212, f32[16,512]{1,0:T(8,128)S(1)} %max.4, pred[512,512]{0,1:T(8,128)(4,1)S(1)} %broadcast_compare_fusion), kind=kLoop, calls=%fused_computation.3 | loop fusion | flops 16769024 | bytes 17104896 | tf_op jit(solution)/shard_map/while/body/eval_jaxpr/cond/branch_1_fun/reduce_sum | solution.py:87
  345.1 11.7 %multiply_add_fusion = f32[16,512,128]{2,1,0:T(8,128)} fusion(f32[16,512,128]{2,1,0:T(8,128)} %get-tuple-element.111, f32[16,512]{1,0:T(8,128)S(1)} %get-tuple-element.210, bf16[4,512,16,128]{3,1,2,0:T(8,128)(2,1)} %get-tuple-element.118, s32[]{:T(128)} %get-tuple-element.116, f32[16,512,512]{2,1,0:T(8,128)} %get-tuple-element.212, f32[16,512]{1,0:T(8,128)S(1)} %max.4, ...), kind=kOutput, calls=%fused_computation.11 | convolution fusion | flops 1092616192 | bytes 27591168 | tf_op jit(solution)/shard_map/while/body/eval_jaxpr/cond/branch_1_fun/hqk,khd->hqd/dot_general | solution.py:88
  368.8 26.1 %fusion.25 = bf16[8192,512]{0,1:T(8,128)(2,1)} fusion(bf16[512,2048]{0,1:T(8,128)(2,1)S(1)} %bitcast.74, bf16[2048,8192]{1,0:T(8,128)(2,1)} %param.15), kind=kOutput, calls=%fused_computation.29 | convolution fusion | flops 17184063488 | bytes 44040192 | tf_op jit(solution)/shard_map/dot_general | solution.py:112
  395.0 234.0 %reduce-scatter.2.cloned.1.call-done = bf16[2048,512]{0,1:T(8,128)(2,1)} async-done(((bf16[8192,512]{0,1:T(8,128)(2,1)}), bf16[2048,512]{0,1:T(8,128)(2,1)}) %reduce-scatter.2.cloned.1.call-update) | async-done | bytes 2097168 | tf_op jit(solution)/shard_map/reduce_scatter | solution.py:111
  (55 shorter events, 62.1 us)
Async XLA Ops:
  7.2 244.3 %all-gather.3.cloned.1.call-start = ((), (), s32[]{:S(2)}) async-start(), calls=%async_computation.1 | async-start | bytes 10485760 | tf_op jit(solution)/shard_map/all_gather | solution.py:63
  8.1 19.4 %collective-permute-start = (bf16[2,3,2048]{2,0,1:T(2,128)(2,1)S(1)}, bf16[2,3,2048]{2,0,1:T(2,128)(2,1)S(1)}, u32[]{:S(2)}, u32[]{:S(2)}) collective-permute-start(bf16[2,3,2048]{2,0,1:T(2,128)(2,1)S(1)} %slice.18), channel_id=1, source_target_pairs={{0,8},{8,16},{16,24},{1,9},{9,17},{17,25},{2,10},{10,18},{18,26},{... | collective-permute-start | bytes 73736 | tf_op jit(solution)/shard_map/ppermute | solution.py:13
  10.5 293.8 %all-gather.5.cloned.1.call-start = ((), (), s32[]{:S(2)}) async-start(), calls=%async_computation.2 | async-start | bytes 10485760 | tf_op jit(solution)/shard_map/all_gather | solution.py:64
  72.7 17.8 %copy-start.4 = (pred[8,65]{0,1:T(8,128)(4,1)S(1)}, pred[8,65]{0,1:T(8,128)(4,1)}, u32[]{:S(2)}) copy-start(pred[8,65]{0,1:T(8,128)(4,1)} %constant.55) | copy-start | bytes 1564
  154.0 14.1 %copy-start.2 = (f32[128,2048]{1,0:T(8,128)S(1)}, f32[128,2048]{1,0:T(8,128)}, u32[]{:S(2)}) copy-start(f32[128,2048]{1,0:T(8,128)} %param.12) | copy-start | bytes 3145732
  162.8 16.0 %collective-permute-start.1 = (bf16[127,2048]{0,1:T(8,128)(2,1)}, bf16[127,2048]{0,1:T(8,128)(2,1)}, u32[]{:S(2)}, u32[]{:S(2)}) collective-permute-start(bf16[127,2048]{0,1:T(8,128)(2,1)} %slice_bitcast_fusion), channel_id=1, source_target_pairs={{0,8},{8,16},{16,24},{1,9},{9,17},{17,25},{2,10},{10,18},{18,26},{... | collective-permute-start | bytes 1560584 | tf_op jit(solution)/shard_map/ppermute | solution.py:13
  178.8 15.6 %copy-start.3 = (f32[128,2048]{1,0:T(8,128)S(1)}, f32[128,2048]{1,0:T(8,128)}, u32[]{:S(2)}) copy-start(f32[128,2048]{1,0:T(8,128)} %rev.7) | copy-start | bytes 3145732
  194.4 48.5 %copy-start = (f32[512,1,2048]{2,0,1:T(8,128)S(1)}, f32[512,1,2048]{2,0,1:T(8,128)}, u32[]{:S(2)}) copy-start(f32[512,1,2048]{2,0,1:T(8,128)} %copy.33) | copy-start | bytes 12582916
  242.9 2.8 copy-start.1
  245.6 383.4 %reduce-scatter.2.cloned.1.call-start = ((), (), s32[]{:S(2)}) async-start(), calls=%async_computation.3 | async-start | bytes 10485760 | tf_op jit(solution)/shard_map/reduce_scatter | solution.py:111
Sparse Core Ops, SparseCore 0:
  10.6 60.8 all-gather.2
  245.7 58.5 all-gather.4
  395.1 233.8 reduce-scatter.1
where the time goes:
time: 644 us; the launch traced here: 636 us
  waiting for transfers between devices  267 us (41%)
  local copies, waits for them, and re-layouts  202 us (31%)
  matrix products  107 us (17%)
  other arithmetic  34.5 us (5%)
  between operations  14.4 us (2%)
  starting transfers between devices  7.87 us (1%)
    reduce_scatter x1, waiting for transfers between devices, per_device(): lax.psum_scatter(lax.dot_general(out_weight, attended, (((0,), (1,)), (()...  234 us
    conv_general_dilated x7, local copies, waits for them, and re-layouts, causal_depthwise(): lax.conv_general_dilated(window[None], kernel, (1,), 'VALID', feature_gro...  90.1 us
    conv_general_dilated x2, matrix products, causal_depthwise(): lax.conv_general_dilated(window[None], kernel, (1,), 'VALID', feature_gro...  60.3 us
    unnamed x17, local copies, waits for them, and re-layouts  49.5 us
    all_gather x1, waiting for transfers between devices, per_device(): value_piece = lax.all_gather(hyena_out, 'seq', axis=0, tiled=True)  33.2 us
    dot_general x1, matrix products, per_device(): lax.dot_general(out_weight, attended, (((0,), (1,)), ((), ())), preferred...  26.1 us
    rev x2, local copies, waits for them, and re-layouts, causal_depthwise(): kernel = taps[::-1][:, None, :]  22.1 us
  transfers between devices with their start and end apart: 5, of which 2 were waited for; matrix products, arithmetic and copies ran while one was open for 40% of the time, Pallas kernels for 0%

commit v1 on v0

--- a/solution.py
+++ b/solution.py
@@ -5,6 +5,28 @@
 from jax.sharding import PartitionSpec as P
 
 HEAD_SIZE = 128
+
+
+def in_order(blocks, dim):
+    blocks = jnp.moveaxis(blocks, 0, dim)
+    shape = blocks.shape
+    return blocks.reshape(*shape[:dim], shape[dim] * shape[dim + 1], *shape[dim + 2 :])
+
+
+def gather_around(array, axis, dim):
+    count = lax.axis_size(axis)
+    pairs = [(i, (i + 1) % count) for i in range(count)]
+    back = [(b, a) for a, b in pairs]
+    lower, upper = ([], [])
+    for step in range(count - 1):
+        if step % 2 == 0:
+            lower.append(lax.ppermute(lower[-1] if lower else array, axis, pairs))
+        else:
+            upper.append(lax.ppermute(upper[-1] if upper else array, axis, back))
+    blocks = jnp.stack([*lower[::-1], array, *upper])
+    shift = lax.axis_index(axis) - len(lower)
+    blocks = blocks[(jnp.arange(count) - shift) % count]
+    return in_order(blocks, dim)
 
 
 def passed_along(x, axis, by):
@@ -61,7 +83,7 @@
     carried = initial
     first_row = jnp.int32(0)
     key_piece = lax.all_gather(k_proj, "seq", axis=0, tiled=True)
-    value_piece = lax.all_gather(hyena_out, "seq", axis=0, tiled=True)
+    value_piece = gather_around(hyena_out, "seq", 0)
     piece_rows = key_piece.shape[0]
     block_rows = math.gcd(piece_rows, 512)
     block_count = piece_rows // block_rows

time: 644 us -> 729 us (1.13)
  local copies, waits for them, and re-layouts: 202 us -> 233 us
  other arithmetic: 34.5 us -> 63.5 us
  waiting for transfers between devices: 267 us -> 287 us
    ppermute x0 -> x3, waiting for transfers between devices: none -> 54.3 us  [the longest x2 54.3 us: gather_around(): lower.append(lax.ppermute(lower[-1] if lower else array, axis, pairs))]
    all_gather x1 -> x0, waiting for transfers between devices: 33.2 us -> none  [per_device(): value_piece = lax.all_gather(hyena_out, 'seq', axis=0, tiled=True)]
    another operation x0 -> x1, other arithmetic: none -> 21.2 us  [gather_around(): blocks = jnp.stack([*lower[::-1], array, *upper])]
    gather x0 -> x5, local copies, waits for them, and re-layouts: none -> 20.7 us  [gather_around(): blocks = blocks[(jnp.arange(count) - shift) % count]]
    another operation x0 -> x3, local copies, waits for them, and re-layouts: none -> 18.4 us  [gather_around(): blocks = jnp.stack([*lower[::-1], array, *upper])]
    unnamed x17 -> x16, local copies, waits for them, and re-layouts: 49.5 us -> 41 us
    unnamed x0 -> x1, other arithmetic: none -> 7.76 us
  transfers between devices with their start and end apart: 5 -> 7, of which waited for: 2 -> 3; matrix products, arithmetic and copies ran while one was open for 40% -> 25% of each run, Pallas kernels for 0% -> 0%
where the time goes in v1:
time: 729 us; the launch traced here: 721 us
  waiting for transfers between devices  287 us (39%)
  local copies, waits for them, and re-layouts  233 us (32%)
  matrix products  110 us (15%)
  other arithmetic  63.5 us (9%)
  between operations  14.4 us (2%)
  starting transfers between devices  9.53 us (1%)
    reduce_scatter x1, waiting for transfers between devices, per_device(): lax.psum_scatter(lax.dot_general(out_weight, attended, (((0,), (1,)), (()...  233 us
    conv_general_dilated x7, local copies, waits for them, and re-layouts, causal_depthwise(): lax.conv_general_dilated(window[None], kernel, (1,), 'VALID', feature_gro...  90.5 us
    conv_general_dilated x2, matrix products, causal_depthwise(): lax.conv_general_dilated(window[None], kernel, (1,), 'VALID', feature_gro...  63.3 us
    ppermute x2, waiting for transfers between devices, gather_around(): lower.append(lax.ppermute(lower[-1] if lower else array, axis, pairs))  54.3 us
    unnamed x16, local copies, waits for them, and re-layouts  41 us
    dot_general x1, matrix products, per_device(): lax.dot_general(out_weight, attended, (((0,), (1,)), ((), ())), preferred...  25.9 us
    rev x2, local copies, waits for them, and re-layouts, causal_depthwise(): kernel = taps[::-1][:, None, :]  22 us
    another operation x1, other arithmetic, gather_around(): blocks = jnp.stack([*lower[::-1], array, *upper])  21.2 us
  transfers between devices with their start and end apart: 7, of which 3 were waited for; matrix products, arithmetic and copies ran while one was open for 25% of the time, Pallas kernels for 0%

profile of v1, /device:TPU:0, one launch (start us, length us, event | category | flops | bytes accessed | tf_op | source)
XLA Modules:
  0.0 721.0 jit_solution(6162801459740739673)
XLA Ops:
  10.5 16.9 %rev.6 = f32[3,6144]{1,0:T(4,128)S(1)} reverse(f32[3,6144]{1,0:T(4,128)} %bitcast.85), dimensions={0} | reverse | bytes 147456 | tf_op jit(solution)/shard_map/rev | solution.py:41
  35.3 9.7 %copy.74 = bf16[514,3,2048]{0,2,1:T(8,128)(2,1)} copy(bf16[514,3,2048]{2,0,1:T(8,128)(2,1)} %pad_maximum_fusion.1) | data formatting | bytes 12632064 | tf_op jit(solution)/shard_map/concatenate | solution.py:62
  52.0 20.5 %reshape.138 = bf16[1,8,65,6144]{2,1,3,0:T(8,128)(2,1)} reshape(bf16[1,520,6144]{1,2,0:T(8,128)(2,1)} %pad) | data formatting | bytes 12779520 | tf_op jit(solution)/shard_map/conv_general_dilated | solution.py:42
  72.5 16.9 %copy.77 = bf16[1,8,65,6144]{3,1,2,0:T(8,128)(2,1)} copy(bf16[1,8,65,6144]{2,1,3,0:T(8,128)(2,1)} %reshape.138) | data formatting | bytes 12779520 | tf_op jit(solution)/shard_map/conv_general_dilated | solution.py:42
  90.3 11.6 %fusion.30 = f32[8,65,6144]{2,0,1:T(8,128)} fusion(f32[3,1,6144]{2,1,0:T(1,128)S(1)} %broadcast_in_dim.41, bf16[1,7,2,6144]{3,1,2,0:T(8,128)(2,1)S(1)} %slice.30, bf16[1,8,65,6144]{3,1,2,0:T(8,128)(2,1)} %copy.77, pred[8,65]{0,1:T(8,128)(4,1)S(1)} %copy-done.4), kind=kOutput, calls=%fused_computation.38 | convolution fusion | flops 137969664 | bytes 19415560 | tf_op jit(solution)/shard_map/conv_general_dilated | solution.py:42
  101.9 17.2 %copy.78 = f32[8,65,6144]{2,1,0:T(8,128)} copy(f32[8,65,6144]{2,0,1:T(8,128)} %fusion.30) | data formatting | bytes 25559040 | tf_op jit(solution)/shard_map/conv_general_dilated | solution.py:42
  119.1 11.3 %reshape.118 = f32[1,520,6144]{2,1,0:T(8,128)} reshape(f32[8,65,6144]{2,1,0:T(8,128)} %copy.78) | data formatting | bytes 25559040 | tf_op jit(solution)/shard_map/conv_general_dilated | solution.py:42
  130.4 10.6 %slice.31 = f32[1,512,6144]{2,1,0:T(8,128)} slice(f32[1,520,6144]{2,1,0:T(8,128)} %reshape.118), slice={[0:1], [0:512], [0:6144]} | slice | bytes 25165824 | tf_op jit(solution)/shard_map/conv_general_dilated | solution.py:42
  140.9 13.1 %copy.79 = f32[1,512,6144]{1,2,0:T(8,128)} copy(f32[1,512,6144]{2,1,0:T(8,128)} %slice.31) | data formatting | bytes 25165824 | tf_op jit(solution)/shard_map/conv_general_dilated | solution.py:42
  173.4 11.3 %copy.101 = f32[512,1,2048]{2,1,0:T(1,128)} copy(f32[512,1,2048]{0,2,1:T(8,128)} %get-tuple-element.245) | data formatting | bytes 8388608
  194.3 11.5 %copy.82 = bf16[1,639,2048]{2,0,1:T(2,128)(2,1)} copy(bf16[1,639,2048]{1,2,0:T(8,128)(2,1)} %maximum_bitcast_fusion.1) | data formatting | bytes 5234688 | tf_op jit(solution)/shard_map/broadcast_in_dim | solution.py:43
  205.8 51.7 %fusion.38 = (bf16[1,512,2048]{2,0,1:T(2,128)(2,1)}, f32[1,512,2048]{2,0,1:T(1,128)S(1)}) fusion(f32[512,1,2048]{2,1,0:T(1,128)} %copy.101, bf16[1,639,2048]{2,0,1:T(2,128)(2,1)} %copy.82, f32[128,1,2048]{2,0,1:T(8,128)S(1)} %bitcast.84), kind=kOutput, calls=%fused_computation.48 | convolution fusion | flops 1612709888 | bytes 14151680 | tf_op jit(solution)/shard_map/conv_general_dilated | solution.py:42
  262.0 45.9 %collective-permute-done.2 = bf16[512,2048]{1,0:T(8,128)(2,1)} collective-permute-done((bf16[512,2048]{1,0:T(8,128)(2,1)}, bf16[512,2048]{1,0:T(8,128)(2,1)}, u32[]{:S(2)}, u32[]{:S(2)}) %collective-permute-start.2) | collective-permute-done | bytes 2097184 | tf_op jit(solution)/shard_map/ppermute | solution.py:23
  325.3 8.4 %collective-permute-done.3 = bf16[512,2048]{1,0:T(8,128)(2,1)} collective-permute-done((bf16[512,2048]{1,0:T(8,128)(2,1)}, bf16[512,2048]{1,0:T(8,128)(2,1)}, u32[]{:S(2)}, u32[]{:S(2)}) %collective-permute-start.3) | collective-permute-done | bytes 2097184 | tf_op jit(solution)/shard_map/ppermute | solution.py:23
  340.5 21.2 %pad_maximum_fusion = bf16[4,512,2048]{2,0,1:T(4,128)(2,1)S(1)} fusion(bf16[1,512,2048]{2,0,1:T(2,128)(2,1)} %copy.87, bf16[1,512,2048]{2,0,1:T(2,128)(2,1)} %get-tuple-element.249, bf16[1,512,2048]{2,0,1:T(2,128)(2,1)S(1)} %copy.86, bf16[1,512,2048]{2,0,1:T(2,128)(2,1)} %copy.85), kind=kLoop, calls=%fused_computation.33 | loop fusion | flops 33554432 | bytes 16777216 | tf_op jit(solution)/shard_map/stack | solution.py:26
  390.2 9.8 %copy.104 = bf16[256,8,16,128]{3,2,1,0:T(8,128)(2,1)} copy(bf16[256,8,16,128]{3,1,2,0:T(8,128)(2,1)} %bitcast.81) | data formatting | bytes 16777216
  400.0 8.8 %copy.90 = bf16[4,512,16,128]{3,1,2,0:T(8,128)(2,1)} copy(bf16[4,512,16,128]{3,2,1,0:T(8,128)(2,1)} %bitcast.78) | data formatting | bytes 16777216
  411.3 35.5 %while.15 = (s32[]{:T(128)}, f32[16,512,128]{2,1,0:T(8,128)}, f32[16,512]{1,0:T(8,128)S(1)}, f32[16,512]{1,0:T(8,128)S(1)}, s32[4]{0:T(128)S(1)}, /*index=5*/s32...) while((s32[]{:T(128)}, f32[16,512,128]{2,1,0:T(8,128)}, ...), condition=%wide.region_5.6_spmd.clone, body=%wide.region_0.5_spmd.clone.sunk | while | flops 2195997696 | bytes 66598184 | solution.py:123
  413.0 29.8 %conditional.3 = ((f32[16,512,128]{2,1,0:T(8,128)}, f32[16,512]{1,0:T(8,128)S(1)}, f32[16,512]{1,0:T(8,128)S(1)})) conditional(s32[]{:T(128)} %convert_element_type.65, (f32[16,512,128]{2,1,0:T(8,128)}, f32[16,512]{1,0:T(8,128)S(1)}, f32[16,512]{1,0:T(8,128)S(1)}) %tuple.51, (s32[]{:T(128)}, s32[]{:T(128)}, bf16[4,512,16,128]{3,1,2,0:T(8,128)(2,1)}, ...), branch_computations={%region_1.1_spmd, %region_2.4_spmd} | conditional | flops 2195997696 | bytes 66595880 | solution.py:121
  413.2 8.8 %fusion.4 = (f32[16,512]{1,0:T(8,128)S(1)}, f32[16,512,512]{2,1,0:T(8,128)}) fusion(pred[512,512]{0,1:T(8,128)(4,1)S(1)} %broadcast_compare_fusion, bf16[512,16,128]{2,0,1:T(8,128)(2,1)S(1)} %get-tuple-element.117, bf16[4,512,16,128]{3,1,2,0:T(8,128)(2,1)} %get-tuple-element.115, s32[]{:T(128)} %get-tuple-element.116), kind=kOutput, calls=%fused_computation.7 | convolution fusion | flops 1086316544 | bytes 21266944 | tf_op jit(solution)/shard_map/while/body/eval_jaxpr/cond/branch_1_fun/qhd,khd->hqk/dot_general | solution.py:100
  422.0 9.1 %fusion.2 = f32[16,512]{1,0:T(8,128)S(1)} fusion(f32[16,512,512]{2,1,0:T(8,128)} %get-tuple-element.242, f32[16,512]{1,0:T(8,128)S(1)} %max.4, pred[512,512]{0,1:T(8,128)(4,1)S(1)} %broadcast_compare_fusion), kind=kLoop, calls=%fused_computation.5 | loop fusion | flops 16769024 | bytes 17104896 | tf_op jit(solution)/shard_map/while/body/eval_jaxpr/cond/branch_1_fun/reduce_sum | solution.py:109
  431.2 11.6 %multiply_add_fusion = f32[16,512,128]{2,1,0:T(8,128)} fusion(f32[16,512,128]{2,1,0:T(8,128)} %get-tuple-element.111, f32[16,512]{1,0:T(8,128)S(1)} %get-tuple-element.240, bf16[4,512,16,128]{3,1,2,0:T(8,128)(2,1)} %get-tuple-element.118, s32[]{:T(128)} %get-tuple-element.116, f32[16,512,512]{2,1,0:T(8,128)} %get-tuple-element.242, f32[16,512]{1,0:T(8,128)S(1)} %max.4, ...), kind=kOutput, calls=%fused_computation.13 | convolution fusion | flops 1092616192 | bytes 27591168 | tf_op jit(solution)/shard_map/while/body/eval_jaxpr/cond/branch_1_fun/hqk,khd->hqd/dot_general | solution.py:110
  454.9 25.9 %fusion.25 = bf16[8192,512]{0,1:T(8,128)(2,1)} fusion(bf16[512,2048]{0,1:T(8,128)(2,1)S(1)} %bitcast.83, bf16[2048,8192]{1,0:T(8,128)(2,1)} %param.15), kind=kOutput, calls=%fused_computation.31 | convolution fusion | flops 17184063488 | bytes 44040192 | tf_op jit(solution)/shard_map/dot_general | solution.py:134
  480.9 233.1 %reduce-scatter.2.cloned.1.call-done = bf16[2048,512]{0,1:T(8,128)(2,1)} async-done(((bf16[8192,512]{0,1:T(8,128)(2,1)}), bf16[2048,512]{0,1:T(8,128)(2,1)}) %reduce-scatter.2.cloned.1.call-update) | async-done | bytes 2097168 | tf_op jit(solution)/shard_map/reduce_scatter | solution.py:133
  (69 shorter events, 118.7 us)
Async XLA Ops:
  7.2 383.0 %all-gather.2.cloned.1.call-start = ((), (), s32[]{:S(2)}) async-start(), calls=%async_computation.1 | async-start | bytes 10485760 | tf_op jit(solution)/shard_map/all_gather | solution.py:85
  8.1 19.3 %collective-permute-start = (bf16[2,3,2048]{2,0,1:T(2,128)(2,1)S(1)}, bf16[2,3,2048]{2,0,1:T(2,128)(2,1)S(1)}, u32[]{:S(2)}, u32[]{:S(2)}) collective-permute-start(bf16[2,3,2048]{2,0,1:T(2,128)(2,1)S(1)} %slice.18), channel_id=1, source_target_pairs={{0,8},{8,16},{16,24},{1,9},{9,17},{17,25},{2,10},{10,18},{18,26},{... | collective-permute-start | bytes 73736 | tf_op jit(solution)/shard_map/ppermute | solution.py:35
  72.5 17.8 %copy-start.4 = (pred[8,65]{0,1:T(8,128)(4,1)S(1)}, pred[8,65]{0,1:T(8,128)(4,1)}, u32[]{:S(2)}) copy-start(pred[8,65]{0,1:T(8,128)(4,1)} %constant.74) | copy-start | bytes 1564
  154.1 14.2 %copy-start.2 = (f32[128,2048]{1,0:T(8,128)S(1)}, f32[128,2048]{1,0:T(8,128)}, u32[]{:S(2)}) copy-start(f32[128,2048]{1,0:T(8,128)} %param.12) | copy-start | bytes 3145732
  162.8 27.4 %collective-permute-start.1 = (bf16[127,2048]{0,1:T(8,128)(2,1)}, bf16[127,2048]{0,1:T(8,128)(2,1)}, u32[]{:S(2)}, u32[]{:S(2)}) collective-permute-start(bf16[127,2048]{0,1:T(8,128)(2,1)} %slice_bitcast_fusion), channel_id=1, source_target_pairs={{0,8},{8,16},{16,24},{1,9},{9,17},{17,25},{2,10},{10,18},{18,26},{... | collective-permute-start | bytes 1560584 | tf_op jit(solution)/shard_map/ppermute | solution.py:35
  168.2 545.8 %reduce-scatter.2.cloned.1.call-start = ((), (), s32[]{:S(2)}) async-start(), calls=%async_computation.2 | async-start | bytes 10485760 | tf_op jit(solution)/shard_map/reduce_scatter | solution.py:133
  190.2 15.6 %copy-start.3 = (f32[128,2048]{1,0:T(8,128)S(1)}, f32[128,2048]{1,0:T(8,128)}, u32[]{:S(2)}) copy-start(f32[128,2048]{1,0:T(8,128)} %rev.7) | copy-start | bytes 3145732
  205.8 51.7 %copy-start = (f32[512,1,2048]{2,0,1:T(8,128)S(1)}, f32[512,1,2048]{2,0,1:T(8,128)}, u32[]{:S(2)}) copy-start(f32[512,1,2048]{2,0,1:T(8,128)} %copy.99) | copy-start | bytes 12582916
  257.5 50.4 %copy-start.1 = (bf16[512,2048]{1,0:T(8,128)(2,1)S(1)}, bf16[512,2048]{1,0:T(8,128)(2,1)}, u32[]{:S(2)}) copy-start(bf16[512,2048]{1,0:T(8,128)(2,1)} %param.13) | copy-start | bytes 6291460
  260.3 47.7 %collective-permute-start.2 = (bf16[512,2048]{1,0:T(8,128)(2,1)}, bf16[512,2048]{1,0:T(8,128)(2,1)}, u32[]{:S(2)}, u32[]{:S(2)}) collective-permute-start(bf16[512,2048]{1,0:T(8,128)(2,1)} %fusion.37), channel_id=1, source_target_pairs={{0,8},{8,16},{16,24},{24,0},{1,9},{9,17},{17,25},{25,1},{2,10},{10... | collective-permute-start | bytes 6291464 | tf_op jit(solution)/shard_map/ppermute | solution.py:23
  260.3 58.2 %collective-permute-start.4 = (bf16[512,2048]{1,0:T(8,128)(2,1)}, bf16[512,2048]{1,0:T(8,128)(2,1)}, u32[]{:S(2)}, u32[]{:S(2)}) collective-permute-start(bf16[512,2048]{1,0:T(8,128)(2,1)} %fusion.37), channel_id=1, source_target_pairs={{8,0},{16,8},{24,16},{0,24},{9,1},{17,9},{25,17},{1,25},{10,2},{18... | collective-permute-start | bytes 6291464 | tf_op jit(solution)/shard_map/ppermute | solution.py:25
  307.9 25.8 %collective-permute-start.3 = (bf16[512,2048]{1,0:T(8,128)(2,1)}, bf16[512,2048]{1,0:T(8,128)(2,1)}, u32[]{:S(2)}, u32[]{:S(2)}) collective-permute-start(bf16[512,2048]{1,0:T(8,128)(2,1)} %collective-permute-done.2), channel_id=1, source_target_pairs={{0,8},{8,16},{16,24},{24,0},{1,9},{9,17},{17,25},{25,1},{2,10},{10... | collective-permute-start | bytes 6291464 | tf_op jit(solution)/shard_map/ppermute | solution.py:23
Sparse Core Ops, SparseCore 0:
  168.3 58.5 all-gather.1
  481.0 232.9 reduce-scatter.1
